TPU v7x, 32 devices: a whole 2x2x4 slice. The times are simulated.
32 devices in a mesh: lat: 4 (over z), lon: 8 (over y, x, core).
Axes of the slice: x: 2, y: 2, z: 4, core: 2. Of those that a mesh axis runs over, the one named last changes fastest.
Arguments:
- grid_nodes: bfloat16 [32768, 512], P(('lat', 'lon')), may hold values from -6 to 6
- grid_edges: bfloat16 [9216, 512], P(('lat', 'lon')), may hold values from -6 to 6
- grid_sender: int32 [9216], P(('lat', 'lon')), may hold values from 0 to 1023
- owner_index: int32 [9216], P(('lat', 'lon')), may hold values from -1 to 255, as said below
- mesh_nodes: bfloat16 [8192, 512], P(('lat', 'lon')), may hold values from -6 to 6
- mesh_edges: bfloat16 [16384, 512], P(('lat', 'lon')), may hold values from -6 to 6
- mesh_sender: int32 [16384], P(('lat', 'lon')), may hold values from 0 to 639
- mesh_receiver: int32 [16384], P(('lat', 'lon')), may hold values from 0 to 255
- w_first: bfloat16 [3, 1536, 512], replicated, may hold values from -0.15625 to 0.15625
- first_bias: float32 [3, 512], replicated, may hold values from -3 to 3
- w_second: bfloat16 [3, 512, 512], replicated, may hold values from -0.25 to 0.25
- norm_gain: float32 [3, 512], replicated, may hold values from 0.25 to 1.75
- mesh_cotangent: bfloat16 [8192, 512], P(('lat', 'lon')), may hold values from -0.0390625 to 0.0390625
- edge_cotangent: bfloat16 [16384, 512], P(('lat', 'lon')), may hold values from -0.0390625 to 0.0390625
Outputs:
- updated_mesh: bfloat16 [8192, 512], P(('lat', 'lon'))
- updated_edges: bfloat16 [16384, 512], P(('lat', 'lon'))
- grad_first: float32 [3, 1536, 512], P(None, 'lat', 'lon')
- grad_second: float32 [3, 512, 512], P(None, 'lat', 'lon')
Inputs may be any that keep to these rules, and one draw needn't show every extreme that they name: `owner_index`: The used slots of a block come first. Blocks from beyond the first or last latitude band are unused. Some device receives 32 used slots from every device that sends to it.
All inputs are finite; a program needn't handle non-finite values.
Results may differ from a plain program's by a relative error of at most 0.02.
Values may be sent and summed in bfloat16 or wider, within the bound.
A program may use at most 128 MiB of HBM per device.

v0:
```python
import jax
import jax.numpy as jnp
from jax import lax
from jax.sharding import PartitionSpec as P

BORDER = 64
K_COARSE = 4


EPSILON = 1e-05


def with_halo(cells, sides, width, closed):
    for axis, dim in sides:
        count = lax.axis_size(axis)
        ends = count if closed else count - 1
        head = lax.slice_in_dim(cells, 0, width, axis=dim)
        tail = lax.slice_in_dim(cells, cells.shape[dim] - width, cells.shape[dim], axis=dim)
        cells = jnp.concatenate(
            [
                lax.ppermute(tail, axis, [(i, (i + 1) % count) for i in range(ends)]),
                cells,
                lax.ppermute(head, axis, [((i + 1) % count, i) for i in range(ends)]),
            ],
            axis=dim,
        )
    return cells


def perceptron(inputs, weights, member, pre_shift, out_shift):
    w_first, first_bias, w_second, norm_gain = weights
    preact = (
        jnp.dot(inputs, w_first[member], preferred_element_type=jnp.float32)
        + first_bias[member]
        + pre_shift
    )
    hidden = jax.nn.silu(preact).astype(jnp.bfloat16)
    output = jnp.dot(hidden, w_second[member], preferred_element_type=jnp.float32) + out_shift
    centre = jnp.mean(output, axis=-1, keepdims=True)
    spread = jnp.mean(jnp.square(output - centre), axis=-1, keepdims=True)
    return ((output - centre) * lax.rsqrt(spread + EPSILON) * norm_gain[member], hidden)


def node_sums(receivers, messages, node_count):
    onehot = (receivers[:, None] == jnp.arange(node_count, dtype=jnp.int32)[None, :]).astype(
        jnp.bfloat16
    )
    summed = lax.dot_general(
        onehot, messages, (((0,), (0,)), ((), ())), preferred_element_type=jnp.float32
    )
    return summed.astype(jnp.bfloat16)


def layer_pass(
    sender_grid,
    grid_edge_rows,
    owner_rows,
    own_nodes,
    sender_table,
    edge_rows,
    edge_senders,
    edge_receivers,
    weights,
    shifts,
):
    node_count = own_nodes.shape[0]
    clipped = jnp.maximum(owner_rows, 0)
    grid_input = jnp.concatenate(
        [grid_edge_rows, sender_grid, jnp.take(own_nodes, clipped, axis=0)], axis=1
    )
    grid_message, grid_hidden = perceptron(grid_input, weights, 0, shifts[0], shifts[1])
    grid_sum = node_sums(owner_rows, grid_message.astype(jnp.bfloat16), node_count)
    edge_input = jnp.concatenate(
        [
            edge_rows,
            jnp.take(sender_table, edge_senders, axis=0),
            jnp.take(own_nodes, edge_receivers, axis=0),
        ],
        axis=1,
    )
    edge_message, edge_hidden = perceptron(edge_input, weights, 1, shifts[2], shifts[3])
    updated_edges = (edge_rows.astype(jnp.float32) + edge_message).astype(jnp.bfloat16)
    edge_sum = node_sums(edge_receivers, edge_message.astype(jnp.bfloat16), node_count)
    node_input = jnp.concatenate([own_nodes, grid_sum, edge_sum], axis=1)
    node_output, node_hidden = perceptron(node_input, weights, 2, shifts[4], shifts[5])
    updated_mesh = (own_nodes.astype(jnp.float32) + node_output).astype(jnp.bfloat16)
    stored = ((grid_input, grid_hidden), (edge_input, edge_hidden), (node_input, node_hidden))
    return ((updated_mesh, updated_edges), stored)


def forward_backward(
    sender_grid,
    grid_edge_rows,
    owner_rows,
    own_nodes,
    sender_table,
    edge_rows,
    edge_senders,
    edge_receivers,
    weights,
    mesh_cot,
    edge_cot,
):
    feature_width = own_nodes.shape[1]
    row_counts = (
        owner_rows.shape[0],
        owner_rows.shape[0],
        edge_senders.shape[0],
        edge_senders.shape[0],
        own_nodes.shape[0],
        own_nodes.shape[0],
    )
    shifts = tuple((jnp.zeros((row_count, feature_width), jnp.float32) for row_count in row_counts))

    def run_layer(shift_list):
        return layer_pass(
            sender_grid,
            grid_edge_rows,
            owner_rows,
            own_nodes,
            sender_table,
            edge_rows,
            edge_senders,
            edge_receivers,
            weights,
            shift_list,
        )

    outputs, pullback, stored = jax.vjp(run_layer, shifts, has_aux=True)
    shift_grads = pullback((mesh_cot, edge_cot))[0]
    firsts = []
    seconds = []
    for member in range(3):
        inputs, hidden = stored[member]
        pre_grad = shift_grads[2 * member].astype(jnp.bfloat16)
        out_grad = shift_grads[2 * member + 1].astype(jnp.bfloat16)
        firsts.append(
            lax.dot_general(
                inputs, pre_grad, (((0,), (0,)), ((), ())), preferred_element_type=jnp.float32
            )
        )
        seconds.append(
            lax.dot_general(
                hidden, out_grad, (((0,), (0,)), ((), ())), preferred_element_type=jnp.float32
            )
        )
    return (outputs[0], outputs[1], jnp.stack(firsts), jnp.stack(seconds))


def shards(
    grid_nodes,
    grid_edges,
    grid_sender,
    owner_index,
    mesh_nodes,
    mesh_edges,
    mesh_sender,
    mesh_receiver,
    w_first,
    first_bias,
    w_second,
    norm_gain,
    mesh_cotangent,
    edge_cotangent,
):
    feature_width = grid_nodes.shape[1]
    slot_count = grid_sender.shape[0]
    per_block = slot_count // 9
    sender_rows = jnp.take(grid_nodes, grid_sender, axis=0)
    packed = jnp.concatenate([grid_edges, sender_rows], axis=1).reshape(
        3, 3, per_block, 2 * feature_width
    )
    padded = with_halo(packed, (("lat", 0), ("lon", 1)), 1, True)
    arrived = padded[0::2, 0::2]
    arrived = arrived.reshape(slot_count, 2 * feature_width)
    border = mesh_nodes[:BORDER][None]
    band_sides = with_halo(border, (("lat", 0),), 1, False)
    cycle_sides = with_halo(border, (("lon", 0),), 1, True)
    coarse = lax.all_gather(
        mesh_nodes[mesh_nodes.shape[0] - K_COARSE :], ("lat", "lon"), axis=0, tiled=True
    )
    sender_table = jnp.concatenate(
        [mesh_nodes, band_sides[0], band_sides[2], cycle_sides[0], cycle_sides[2], coarse], axis=0
    )
    weights = (w_first, first_bias, w_second, norm_gain)
    updated_mesh, updated_edges, first_term, second_term = forward_backward(
        arrived[:, feature_width:],
        arrived[:, :feature_width],
        owner_index,
        mesh_nodes,
        sender_table,
        mesh_edges,
        mesh_sender,
        mesh_receiver,
        weights,
        mesh_cotangent,
        edge_cotangent,
    )
    banded = (
        lax.psum_scatter(
            first_term.astype(jnp.bfloat16), "lat", scatter_dimension=1, tiled=True
        ).astype(jnp.float32),
        lax.psum_scatter(
            second_term.astype(jnp.bfloat16), "lat", scatter_dimension=1, tiled=True
        ).astype(jnp.float32),
    )
    grad_first, grad_second = (
        lax.psum_scatter(
            banded[0].astype(jnp.bfloat16), "lon", scatter_dimension=2, tiled=True
        ).astype(jnp.float32),
        lax.psum_scatter(
            banded[1].astype(jnp.bfloat16), "lon", scatter_dimension=2, tiled=True
        ).astype(jnp.float32),
    )
    return (updated_mesh, updated_edges, grad_first, grad_second)


def solution(mesh):
    return jax.shard_map(
        shards,
        mesh=mesh,
        in_specs=(
            P(("lat", "lon"), None),
            P(("lat", "lon"), None),
            P(("lat", "lon")),
            P(("lat", "lon")),
            P(("lat", "lon"), None),
            P(("lat", "lon"), None),
            P(("lat", "lon")),
            P(("lat", "lon")),
            P(),
            P(),
            P(),
            P(),
            P(("lat", "lon"), None),
            P(("lat", "lon"), None),
        ),
        out_specs=(
            P(("lat", "lon"), None),
            P(("lat", "lon"), None),
            P(None, "lat", "lon"),
            P(None, "lat", "lon"),
        ),
        check_vma=False,
    )
```

profile of v0, /device:TPU:0, one launch (start us, length us, event | category | flops | bytes accessed | tf_op | source)
XLA Modules:
  0.0 308.2 jit_solution(8122458618943222096)
XLA Ops:
  8.2 3.3 %collective-permute-start.7 = (bf16[1,64,512]{2,1,0:T(8,128)(2,1)S(1)}, bf16[1,64,512]{2,1,0:T(8,128)(2,1)S(1)}, u32[]{:S(2)}, u32[]{:S(2)}) collective-permute-start(bf16[1,64,512]{2,1,0:T(8,128)(2,1)S(1)} %slice_bitcast_fusion), channel_id=1, source_target_pairs={{1,0},{2,1},{3,2},{4,3},{5,4},{6,5},{7,6},{0,7},{9,8},{10,9},{11,1... | collective-permute-start | bytes 196616 | tf_op jit(solution)/shard_map/ppermute | solution.py:23
  12.8 5.2 %collective-permute-start.4 = (bf16[1,64,512]{2,1,0:T(8,128)(2,1)S(1)}, bf16[1,64,512]{2,1,0:T(8,128)(2,1)}, u32[]{:S(2)}, u32[]{:S(2)}) collective-permute-start(bf16[1,64,512]{2,1,0:T(8,128)(2,1)S(1)} %slice_bitcast_fusion), channel_id=1, source_target_pairs={{0,8},{8,16},{16,24},{1,9},{9,17},{17,25},{2,10},{10,18},{18,26},{... | collective-permute-start | bytes 196616 | tf_op jit(solution)/shard_map/ppermute | solution.py:21
  19.4 2.0 gather_fusion
  22.3 1.4 collective-permute-start.1
  25.2 39.8 %all-gather = bf16[32,4,512]{2,1,0:T(4,128)(2,1)S(1)} all-gather(bf16[1,4,512]{2,1,0:T(4,128)(2,1)S(1)} %slice_bitcast_fusion.1), channel_id=1, replica_groups=mesh['lat'=4,'lon'=8] {'lat','lon'}, dimensions={0}, use_global_device_ids=true | all-gather | bytes 135168 | tf_op jit(solution)/shard_map/all_gather | solution.py:179
  65.6 2.0 gather_fusion.1
  67.6 2.6 gather_fusion.3
  71.5 2.1 copy.23
  74.4 2.0 broadcast_select_fusion
  79.0 2.6 gather_fusion.2
  82.9 2.9 fusion.14
  88.1 2.3 collective-permute-start.3
  91.0 4.8 %collective-permute-done.2 = bf16[5,1,32,1024]{3,2,1,0:T(8,128)(2,1)S(1)} collective-permute-done((bf16[5,1,32,1024]{3,2,1,0:T(8,128)(2,1)S(1)}, bf16[5,1,32,1024]{3,2,1,0:T(8,128)(2,1)S(1)}, u32[]{:S(2)}, u32[]{:S(2)}) %collective-permute-start.2) | collective-permute-done | bytes 327712 | tf_op jit(solution)/shard_map/ppermute | solution.py:21
  104.5 1.5 multiply_reduce_fusion.3
  107.9 1.3 pad_maximum_fusion.3
  110.3 2.7 fusion.1
  113.0 4.4 %fusion = bf16[1,1536,512]{2,1,0:T(8,128)(2,1)} fusion(f32[288,512]{1,0:T(8,128)} %copy-done.28, bf16[288,512]{1,0:T(8,128)(2,1)} %broadcast_select_fusion.2, bf16[288,1024]{1,0:T(8,128)(2,1)} %bitcast.82, bf16[3,512,512]{2,1,0:T(8,128)(2,1)} %param.24, f32[288,512]{1,0:T(8,128)} %copy-done.8, f32[288,512]{1,0:T(8,128)S(1)} %get-tuple-element.39, ...), kind=kOutput, calls=%fused_computation.8 | convolution fusion | flops 609042432 | bytes 4755968 | tf_op jit(solution)/shard_map/dot_general | solution.py:138
  117.4 4.7 %fusion.2 = bf16[1,1536,512]{2,1,0:T(8,128)(2,1)} fusion(f32[512,512]{1,0:T(8,128)} %copy-done.29, bf16[512,512]{1,0:T(8,128)(2,1)} %broadcast_select_fusion, bf16[512,512]{1,0:T(8,128)(2,1)} %copy-done.11, bf16[512,512]{1,0:T(8,128)(2,1)S(1)} %copy-done.9, bf16[3,512,512]{2,1,0:T(8,128)(2,1)} %param.24, f32[512,512]{0,1:T(8,128)} %copy-done.5, ...), kind=kOutput, calls=%fused_computation.10 | convolution fusion | flops 1083703296 | bytes 6823936 | tf_op jit(solution)/shard_map/dot_general | solution.py:138
  122.2 5.0 %pad_maximum_fusion = bf16[3,1536,512]{2,1,0:T(8,128)(2,1)} fusion(bf16[1,1536,512]{2,1,0:T(8,128)(2,1)} %fusion.1, bf16[1,1536,512]{2,1,0:T(8,128)(2,1)} %fusion.2, bf16[1,1536,512]{2,1,0:T(8,128)(2,1)} %fusion), kind=kLoop, calls=%fused_computation.4 | loop fusion | flops 4718592 | bytes 9437184 | tf_op jit(solution)/shard_map/stack | solution.py:147
  127.3 18.7 %reduce-scatter.5.cloned.1.call-done = bf16[3,128,512]{2,1,0:T(8,128)(2,1)} async-done(((bf16[3,512,512]{2,1,0:T(8,128)(2,1)}), bf16[3,128,512]{2,1,0:T(8,128)(2,1)}) %reduce-scatter.5.cloned.1.call-update) | async-done | bytes 393232 | tf_op jit(solution)/shard_map/reduce_scatter | solution.py:203
  146.0 2.1 copy.26
  148.1 84.5 %reduce-scatter.3.cloned.1.call-done = bf16[3,384,512]{2,1,0:T(8,128)(2,1)} async-done(((bf16[3,1536,512]{2,1,0:T(8,128)(2,1)}), bf16[3,384,512]{2,1,0:T(8,128)(2,1)}) %reduce-scatter.3.cloned.1.call-update) | async-done | bytes 1179664 | tf_op jit(solution)/shard_map/reduce_scatter | solution.py:200
  232.5 3.6 %copy.25 = bf16[3,384,512]{1,0,2:T(4,128)(2,1)} copy(bf16[3,384,512]{2,1,0:T(8,128)(2,1)} %reduce-scatter.3.cloned.1.call-done) | data formatting | bytes 2359296 | tf_op jit(solution)/shard_map/reduce_scatter | solution.py:200
  239.1 59.3 %all-reduce.5.cloned.1.call-done = (bf16[3,384,512]{1,0,2:T(4,128)(2,1)}, bf16[3,128,512]{1,0,2:T(4,128)(2,1)}) async-done(((bf16[3,384,512]{1,0,2:T(4,128)(2,1)}, bf16[3,128,512]{1,0,2:T(4,128)(2,1)}), (bf16[3,384,512]{1,0,2:T(4,128)(2,1)}, bf16[3,128,512]{1,0,2:T(4,128)(2,1)})) %all-reduce.5.cloned.1.call-update) | async-done | bytes 1572880
  (149 shorter events, 32.1 us)
Async XLA Ops:
  7.2 12.2 %copy-start = (bf16[1024,512]{1,0:T(8,128)(2,1)S(1)}, bf16[1024,512]{1,0:T(8,128)(2,1)}, u32[]{:S(2)}) copy-start(bf16[1024,512]{1,0:T(8,128)(2,1)} %param.14) | copy-start | bytes 3145732
  7.2 138.8 %reduce-scatter.5.cloned.1.call-start = ((), (), s32[]{:S(2)}) async-start(), calls=%async_computation.3 | async-start | bytes 1966080 | tf_op jit(solution)/shard_map/reduce_scatter | solution.py:203
  8.2 70.8 %collective-permute-start.7 = (bf16[1,64,512]{2,1,0:T(8,128)(2,1)S(1)}, bf16[1,64,512]{2,1,0:T(8,128)(2,1)S(1)}, u32[]{:S(2)}, u32[]{:S(2)}) collective-permute-start(bf16[1,64,512]{2,1,0:T(8,128)(2,1)S(1)} %slice_bitcast_fusion), channel_id=1, source_target_pairs={{1,0},{2,1},{3,2},{4,3},{5,4},{6,5},{7,6},{0,7},{9,8},{10,9},{11,1... | collective-permute-start | bytes 196616 | tf_op jit(solution)/shard_map/ppermute | solution.py:23
  11.5 66.7 %collective-permute-start.6 = (bf16[1,64,512]{2,1,0:T(8,128)(2,1)S(1)}, bf16[1,64,512]{2,1,0:T(8,128)(2,1)}, u32[]{:S(2)}, u32[]{:S(2)}) collective-permute-start(bf16[1,64,512]{2,1,0:T(8,128)(2,1)S(1)} %slice_bitcast_fusion), channel_id=1, source_target_pairs={{0,1},{1,2},{2,3},{3,4},{4,5},{5,6},{6,7},{7,0},{8,9},{9,10},{10,1... | collective-permute-start | bytes 196616 | tf_op jit(solution)/shard_map/ppermute | solution.py:21
  11.5 65.8 %collective-permute-start.5 = (bf16[1,64,512]{2,1,0:T(8,128)(2,1)S(1)}, bf16[1,64,512]{2,1,0:T(8,128)(2,1)}, u32[]{:S(2)}, u32[]{:S(2)}) collective-permute-start(bf16[1,64,512]{2,1,0:T(8,128)(2,1)S(1)} %slice_bitcast_fusion), channel_id=1, source_target_pairs={{8,0},{16,8},{24,16},{9,1},{17,9},{25,17},{10,2},{18,10},{26,18},{... | collective-permute-start | bytes 196616 | tf_op jit(solution)/shard_map/ppermute | solution.py:23
  12.8 63.6 %collective-permute-start.4 = (bf16[1,64,512]{2,1,0:T(8,128)(2,1)S(1)}, bf16[1,64,512]{2,1,0:T(8,128)(2,1)}, u32[]{:S(2)}, u32[]{:S(2)}) collective-permute-start(bf16[1,64,512]{2,1,0:T(8,128)(2,1)S(1)} %slice_bitcast_fusion), channel_id=1, source_target_pairs={{0,8},{8,16},{16,24},{1,9},{9,17},{17,25},{2,10},{10,18},{18,26},{... | collective-permute-start | bytes 196616 | tf_op jit(solution)/shard_map/ppermute | solution.py:21
  19.4 4.4 %copy-start.15 = (s32[288]{0:T(512)S(1)}, s32[288]{0:T(512)}, u32[]{:S(2)}) copy-start(s32[288]{0:T(512)} %param.17) | copy-start | bytes 3460
  19.4 4.4 %copy-start.16 = (s32[512]{0:T(512)S(1)}, s32[512]{0:T(512)}, u32[]{:S(2)}) copy-start(s32[512]{0:T(512)} %param.21) | copy-start | bytes 6148
  19.4 4.5 %copy-start.1 = (bf16[256,512]{1,0:T(8,128)(2,1)S(1)}, bf16[256,512]{1,0:T(8,128)(2,1)}, u32[]{:S(2)}) copy-start(bf16[256,512]{1,0:T(8,128)(2,1)} %param.18) | copy-start | bytes 786436
  22.3 64.3 %collective-permute-start.1 = (bf16[1,3,32,1024]{3,2,1,0:T(8,128)(2,1)}, bf16[1,3,32,1024]{3,2,1,0:T(8,128)(2,1)}, u32[]{:S(2)}, u32[]{:S(2)}) collective-permute-start(bf16[1,3,32,1024]{3,2,1,0:T(8,128)(2,1)} %bitcast.2), channel_id=1, source_target_pairs={{8,0},{16,8},{24,16},{0,24},{9,1},{17,9},{25,17},{1,25},{10,2},{18... | collective-permute-start | bytes 589832 | tf_op jit(solution)/shard_map/ppermute | solution.py:23
  73.6 5.4 %copy-start.10 = (bf16[128,512]{1,0:T(8,128)(2,1)S(1)}, bf16[128,512]{1,0:T(8,128)(2,1)}, u32[]{:S(2)}) copy-start(bf16[128,512]{1,0:T(8,128)(2,1)} %reshape.158) | copy-start | bytes 393220
  76.4 10.3 %collective-permute-start = (bf16[1,3,32,1024]{3,2,1,0:T(8,128)(2,1)}, bf16[1,3,32,1024]{3,2,1,0:T(8,128)(2,1)}, u32[]{:S(2)}, u32[]{:S(2)}) collective-permute-start(bf16[1,3,32,1024]{3,2,1,0:T(8,128)(2,1)} %bitcast), channel_id=1, source_target_pairs={{0,8},{8,16},{16,24},{24,0},{1,9},{9,17},{17,25},{25,1},{2,10},{10... | collective-permute-start | bytes 589832 | tf_op jit(solution)/shard_map/ppermute | solution.py:21
  82.9 14.3 %slice-start = ((s8[4718592]{0:T(1024)(128)(4,1)}), s8[4194304]{0:T(1024)(128)(4,1)S(1)}, s32[]{:S(2)}) async-start(s8[4718592]{0:T(1024)(128)(4,1)} %bitcast.94), calls=%async_computation.5 | async-start | bytes 8388608
  85.8 21.4 %copy-start.29 = (f32[512,512]{1,0:T(8,128)}, f32[512,512]{1,0:T(8,128)S(1)}, u32[]{:S(2)}) copy-start(f32[512,512]{1,0:T(8,128)S(1)} %fusion.14) | copy-start | bytes 3145732
  85.8 11.3 %slice-start.1 = ((s8[4718592]{0:T(1024)(128)(4,1)}), s8[524288]{0:T(1024)(128)(4,1)S(1)}, s32[]{:S(2)}) async-start(s8[4718592]{0:T(1024)(128)(4,1)} %bitcast.94), calls=%async_computation.6 | async-start | bytes 1048576
  87.7 8.1 %collective-permute-start.2 = (bf16[5,1,32,1024]{3,2,1,0:T(8,128)(2,1)S(1)}, bf16[5,1,32,1024]{3,2,1,0:T(8,128)(2,1)S(1)}, u32[]{:S(2)}, u32[]{:S(2)}) collective-permute-start(bf16[5,1,32,1024]{3,2,1,0:T(8,128)(2,1)S(1)} %get-tuple-element.21), channel_id=1, source_target_pairs={{0,1},{1,2},{2,3},{3,4},{4,5},{5,6},{6,7},{7,0},{8,9},{9,10},{10,1... | collective-permute-start | bytes 983048 | tf_op jit(solution)/shard_map/ppermute | solution.py:21
  88.1 7.7 %collective-permute-start.3 = (bf16[5,1,32,1024]{3,2,1,0:T(8,128)(2,1)S(1)}, bf16[5,1,32,1024]{3,2,1,0:T(8,128)(2,1)S(1)}, u32[]{:S(2)}, u32[]{:S(2)}) collective-permute-start(bf16[5,1,32,1024]{3,2,1,0:T(8,128)(2,1)S(1)} %get-tuple-element.22), channel_id=1, source_target_pairs={{1,0},{2,1},{3,2},{4,3},{5,4},{6,5},{7,6},{0,7},{9,8},{10,9},{11,1... | collective-permute-start | bytes 983048 | tf_op jit(solution)/shard_map/ppermute | solution.py:23
  90.9 8.3 %copy-start.25 = (bf16[256,512]{1,0:T(8,128)(2,1)}, bf16[256,512]{1,0:T(8,128)(2,1)S(1)}, u32[]{:S(2)}) copy-start(bf16[256,512]{1,0:T(8,128)(2,1)S(1)} %convolution_convert_fusion.11) | copy-start | bytes 786436
  91.0 6.2 %copy-start.12 = (bf16[288,512]{1,0:T(8,128)(2,1)S(1)}, bf16[288,512]{1,0:T(8,128)(2,1)}, u32[]{:S(2)}) copy-start(bf16[288,512]{1,0:T(8,128)(2,1)} %broadcast_select_fusion.2) | copy-start | bytes 884740
  91.0 6.2 %copy-start.22 = (f32[1,512]{1,0:T(1,128)S(1)}, f32[1,512]{1,0:T(1,128)}, u32[]{:S(2)}) copy-start(f32[1,512]{1,0:T(1,128)} %get-tuple-element.31) | copy-start | bytes 6148
  98.0 8.5 %copy-start.28 = (f32[288,512]{1,0:T(8,128)}, f32[288,512]{1,0:T(8,128)S(1)}, u32[]{:S(2)}) copy-start(f32[288,512]{1,0:T(8,128)S(1)} %fusion.20) | copy-start | bytes 1769476
  109.3 123.2 %reduce-scatter.3.cloned.1.call-start = ((), (), s32[]{:S(2)}) async-start(), calls=%async_computation.2 | async-start | bytes 5898240 | tf_op jit(solution)/shard_map/reduce_scatter | solution.py:200
  113.0 4.4 %copy-start.9 = (bf16[512,512]{1,0:T(8,128)(2,1)S(1)}, bf16[512,512]{1,0:T(8,128)(2,1)}, u32[]{:S(2)}) copy-start(bf16[512,512]{1,0:T(8,128)(2,1)} %param.19) | copy-start | bytes 1572868
  127.2 171.2 %all-reduce.5.cloned.1.call-start = ((), (), s32[]{:S(2)}) async-start(), calls=%async_computation.4 | async-start | bytes 4194304
  (19 other events, 35.6 us)
Sparse Core Ops, SparseCore 0:
  109.4 36.5 reduce-scatter.4
  148.3 84.1 reduce-scatter.2
  236.3 62.0 all-reduce.4
where the time goes:
time: 309 us; the launch traced here: 308 us
  waiting for transfers between devices  167 us (54%)
  blocking collectives  39.8 us (13%)
  local copies, waits for them, and re-layouts  29.3 us (9%)
  matrix products  23.5 us (8%)
  other arithmetic  19 us (6%)
  between operations  15 us (5%)
  starting transfers between devices  14.1 us (5%)
    reduce_scatter x1, waiting for transfers between devices, shards(): lax.psum_scatter(first_term.astype(jnp.bfloat16), 'lat', scatter_dimensio...  84.5 us
    unnamed x4, waiting for transfers between devices  59.4 us
    all_gather x1, blocking collectives, shards(): lax.all_gather(mesh_nodes[mesh_nodes.shape[0] - K_COARSE:], ('lat', 'lon'...  39.8 us
    reduce_scatter x1, waiting for transfers between devices, shards(): lax.psum_scatter(second_term.astype(jnp.bfloat16), 'lat', scatter_dimensi...  18.7 us
    unnamed x77, local copies, waits for them, and re-layouts  12.2 us
    dot_general x3, matrix products, forward_backward(): lax.dot_general(inputs, pre_grad, (((0,), (0,)), ((), ())), preferred_ele...  11.8 us
    ppermute x4, starting transfers between devices, with_halo(): lax.ppermute(head, axis, [((i + 1) % count, i) for i in range(ends)])  8.31 us
    another operation x2, other arithmetic, forward_backward(): return (outputs[0], outputs[1], jnp.stack(firsts), jnp.stack(seconds))  6.37 us
  transfers between devices with their start and end apart: 11, of which 4 were waited for; matrix products, arithmetic and copies ran while one was open for 16% of the time, Pallas kernels for 0%

commit v1 on v0

v1 whole, which is shorter than its diff:
```python
import functools

import jax
import jax.numpy as jnp
from jax import lax
from jax.experimental import pallas as pl
from jax.experimental.pallas import tpu as pltpu
from jax.sharding import PartitionSpec as P

BORDER = 64
K_COARSE = 4
EPSILON = 1e-05
LANES = 128
MESH = pl.DeviceIdType.MESH
F32 = jnp.float32
BF16 = jnp.bfloat16


def mm(a, b, ca=1, cb=0):
    return lax.dot_general(a, b, (((ca,), (cb,)), ((), ())), preferred_element_type=F32)


def onehot_t(index, count):
    rows = lax.broadcasted_iota(jnp.int32, (count, index.shape[1]), 0)
    return jnp.where(rows == index, 1.0, 0.0).astype(BF16)


def bits_of(count):
    return count.bit_length() - 1


def plan(nlat, nlon, lanes):
    lat = [("lat", b) for b in range(bits_of(nlat))]
    lon = [("lon", b) for b in range(bits_of(nlon))]
    core, rest = lon[:1], lon[1:]
    orders = [
        core + rest + lat,
        core + rest[1:] + lat + rest[:1],
        core + lat + rest,
    ]
    units = lanes // LANES
    if units >= 4:
        cuts = [0, units // 2, 3 * units // 4, units]
    elif units >= 2:
        cuts = [0, units // 2, units]
    else:
        return [(0, lanes, orders[0])]
    return [
        (cuts[i] * LANES, cuts[i + 1] * LANES, orders[i]) for i in range(len(cuts) - 1)
    ]


def kernel(nlat, nlon, groups, *refs):
    (gn, ge, gs, ow, mn, me_h, ms, mr, wf_h, fb, ws_h, ng, mc_h, ec_h) = refs[:14]
    (um, ue, gout) = refs[14:17]
    ngroups = len(groups)
    g_refs = refs[17 : 17 + ngroups]
    r_refs = refs[17 + ngroups : 17 + 2 * ngroups]
    (
        snd, x0, x1, x2, bord, coarse,
        h0, h1, h2, p0, p1, p2, n0, n1, n2, r0, r1, r2,
        pg0, pg1, pg2, og0, og1, og2,
        wf, ws, mc, ec,
        load_sem, slot_send, slot_recv, side_send, side_recv, row_send, row_recv, col_send, col_recv,
        red_send, red_recv,
    ) = refs[17 + 2 * ngroups :]
    xs, hs, ps, ns, rs = (x0, x1, x2), (h0, h1, h2), (p0, p1, p2), (n0, n1, n2), (r0, r1, r2)
    pgs, ogs = (pg0, pg1, pg2), (og0, og1, og2)
    lat, lon = lax.axis_index("lat"), lax.axis_index("lon")
    nodes, d = mn.shape
    slots = ge.shape[0]
    cap = slots // 9
    edges = ue.shape[0]
    has = {-1: lat > 0, 1: lat < nlat - 1}

    def when(a, action):
        if a == 0:
            action()
        else:
            pl.when(has[a])(action)

    loads = [
        pltpu.make_async_copy(wf_h, wf, load_sem.at[0]),
        pltpu.make_async_copy(ws_h, ws, load_sem.at[1]),
        pltpu.make_async_copy(me_h, x1.at[:, pl.ds(0, d)], load_sem.at[2]),
        pltpu.make_async_copy(mc_h, mc, load_sem.at[3]),
        pltpu.make_async_copy(ec_h, ec, load_sem.at[4]),
    ]
    for copy in loads:
        copy.start()

    barrier = pltpu.get_barrier_semaphore()
    peers = [(lat, lax.rem(lon + s, nlon)) for s in range(1, nlon)]
    peers += [(lax.rem(lat + s, nlat), lon) for s in range(1, nlat)]
    peers += [
        (lax.rem(lat + a, nlat), lax.rem(lon + b, nlon))
        for a in (1, nlat - 1)
        for b in (1, nlon - 1)
    ]
    for peer in peers:
        pl.semaphore_signal(barrier, inc=1, device_id=peer, device_id_type=MESH)

    snd[...] = mm(onehot_t(gs[...], gn.shape[0]), gn[...], 0, 0).astype(BF16)
    per_dev = K_COARSE * d // LANES
    tail = mn[nodes - 16 : nodes, :]
    out_row = lax.broadcasted_iota(jnp.int32, (per_dev, 16), 0)
    in_row = lax.broadcasted_iota(jnp.int32, (per_dev, 16), 1)
    staged = jnp.zeros((per_dev, LANES), F32)
    for q in range(d // LANES):
        pick = (out_row - q * K_COARSE == in_row - (16 - K_COARSE)) & (in_row >= 16 - K_COARSE)
        staged += mm(jnp.where(pick, 1.0, 0.0).astype(BF16), tail[:, q * LANES : (q + 1) * LANES])
    me_row = (lat * nlon + lon) * per_dev
    coarse[pl.ds(pl.multiple_of(me_row, 16), per_dev), :] = staged.astype(BF16)

    @pl.when(lat == 0)
    def _():
        x0[0 : 3 * cap, 0 : 2 * d] = jnp.zeros((3 * cap, 2 * d), BF16)
        bord[0:BORDER, :] = jnp.zeros((BORDER, d), BF16)

    @pl.when(lat == nlat - 1)
    def _():
        x0[6 * cap : 9 * cap, 0 : 2 * d] = jnp.zeros((3 * cap, 2 * d), BF16)
        bord[BORDER : 2 * BORDER, :] = jnp.zeros((BORDER, d), BF16)

    pl.semaphore_wait(barrier, len(peers))

    def slot_copy(o, part):
        a, b = o // 3 - 1, o % 3 - 1
        src = (ge, snd)[part]
        return pltpu.make_async_remote_copy(
            src_ref=src.at[pl.ds(o * cap, cap)],
            dst_ref=x0.at[pl.ds((8 - o) * cap, cap), pl.ds(part * d, d)],
            send_sem=slot_send.at[part, o],
            recv_sem=slot_recv.at[part, 8 - o],
            device_id=(lat + a, lax.rem(lon + b + nlon, nlon)),
            device_id_type=MESH,
        )

    def side_copy(side):
        a, b = ((1, 0), (-1, 0), (0, 1), (0, -1))[side]
        return pltpu.make_async_remote_copy(
            src_ref=mn.at[pl.ds(0, BORDER)],
            dst_ref=bord.at[pl.ds(side * BORDER, BORDER)],
            send_sem=side_send.at[side],
            recv_sem=side_recv.at[side],
            device_id=(lat + a, lax.rem(lon + b + nlon, nlon)),
            device_id_type=MESH,
        )

    side_a = (1, -1, 0, 0)
    remote_slots = [o for o in (0, 2, 6, 8, 1, 7, 3, 5)]
    for o in remote_slots:
        when(o // 3 - 1, lambda o=o: slot_copy(o, 1).start())
    for o in remote_slots:
        when(o // 3 - 1, lambda o=o: slot_copy(o, 0).start())

    def row_copy(s):
        from_row = (lat * nlon + lon) * per_dev
        span = pl.ds(pl.multiple_of(from_row, 16), per_dev)
        return pltpu.make_async_remote_copy(
            src_ref=coarse.at[span], dst_ref=coarse.at[span],
            send_sem=row_send.at[s], recv_sem=row_recv.at[s],
            device_id=(lat, lax.rem(lon + s, nlon)), device_id_type=MESH,
        )

    def row_arrival(s):
        owner = lax.rem(lon - s + nlon, nlon)
        span = pl.ds(pl.multiple_of((lat * nlon + owner) * per_dev, 16), per_dev)
        return pltpu.make_async_remote_copy(
            src_ref=coarse.at[span], dst_ref=coarse.at[span],
            send_sem=row_send.at[s], recv_sem=row_recv.at[s],
            device_id=(lat, owner), device_id_type=MESH,
        )

    def col_copy(s, incoming):
        other = lax.rem(lat - s + nlat, nlat) if incoming else lax.rem(lat + s, nlat)
        owner = other if incoming else lat
        span = pl.ds(pl.multiple_of(owner * nlon * per_dev, 16), nlon * per_dev)
        return pltpu.make_async_remote_copy(
            src_ref=coarse.at[span], dst_ref=coarse.at[span],
            send_sem=col_send.at[s], recv_sem=col_recv.at[s],
            device_id=(other, lon), device_id_type=MESH,
        )

    for s in range(1, nlon):
        row_copy(s).start()
    for side in range(4):
        when(side_a[side], lambda side=side: side_copy(side).start())

    x0[4 * cap : 5 * cap, 0:d] = ge[4 * cap : 5 * cap, :]
    x0[4 * cap : 5 * cap, d : 2 * d] = snd[4 * cap : 5 * cap, :]
    own_t = onehot_t(jnp.maximum(ow[...], 0), nodes)
    x0[:, 2 * d : 3 * d] = mm(own_t, mn[...], 0, 0).astype(BF16)
    recv_t = onehot_t(mr[...], nodes)
    x1[:, 2 * d : 3 * d] = mm(recv_t, mn[...], 0, 0).astype(BF16)
    sender = ms[...]
    n1[...] = mm(onehot_t(sender, nodes), mn[...], 0, 0)

    for s in range(1, nlon):
        row_arrival(s).wait_recv()
    for s in range(1, nlat):
        col_copy(s, False).start()
    for copy in loads[:2]:
        copy.wait()

    def forward(k, lo, size):
        rows = pl.ds(lo, size)
        pre = mm(xs[k][rows, :], wf[k]) + fb[k : k + 1, :]
        ps[k][rows, :] = pre
        hidden = (pre * jax.nn.sigmoid(pre)).astype(BF16)
        hs[k][rows, :] = hidden
        out = mm(hidden, ws[k])
        centred = out - jnp.mean(out, axis=-1, keepdims=True)
        scale = lax.rsqrt(jnp.mean(centred * centred, axis=-1, keepdims=True) + EPSILON)
        normed = centred * scale
        ns[k][rows, :] = normed
        rs[k][rows, :] = scale
        return normed * ng[k : k + 1, :]

    def backward(k, lo, size, dmsg):
        rows = pl.ds(lo, size)
        dn = dmsg * ng[k : k + 1, :]
        normed = ns[k][rows, :]
        dout = rs[k][rows, :] * (
            dn
            - jnp.mean(dn, axis=-1, keepdims=True)
            - normed * jnp.mean(dn * normed, axis=-1, keepdims=True)
        )
        og = dout.astype(BF16)
        ogs[k][rows, :] = og
        dh = mm(og, ws[k], 1, 1).astype(BF16).astype(F32)
        pre = ps[k][rows, :]
        gate = jax.nn.sigmoid(pre)
        pg = (dh * (gate * (1.0 + pre * (1.0 - gate)))).astype(BF16)
        pgs[k][rows, :] = pg
        return pg

    def tiles(count):
        size = 256 if count % 256 == 0 else count
        return [(i * size, size) for i in range(count // size)]

    for j in remote_slots:
        def arrive(j=j):
            slot_copy(8 - j, 0).wait_recv()
            slot_copy(8 - j, 1).wait_recv()
        when(j // 3 - 1, arrive)
    grid_msgs = [forward(0, lo, size).astype(BF16) for lo, size in tiles(slots)]
    grid_t = onehot_t(ow[...], nodes)
    x2[:, 0:d] = mn[...]
    total = 0.0
    for (lo, size), msg in zip(tiles(slots), grid_msgs):
        total += mm(grid_t[:, lo : lo + size], msg)
    x2[:, d : 2 * d] = total.astype(BF16)

    for side in range(4):
        when(-side_a[side], lambda side=side: side_copy(side).wait_recv())
    n1[...] += mm(onehot_t(sender - nodes, 4 * BORDER), bord[...], 0, 0)
    for s in range(1, nlat):
        col_copy(s, True).wait_recv()
    rank = sender - (nodes + 4 * BORDER)
    place = lax.shift_right_logical(rank, 2) * per_dev + (rank & (K_COARSE - 1))
    for q in range(d // LANES):
        target = jnp.where(rank >= 0, place + q * K_COARSE, -1)
        picked = mm(onehot_t(target, coarse.shape[0]), coarse[...], 0, 0)
        span = slice(q * LANES, (q + 1) * LANES)
        x1[:, d + q * LANES : d + (q + 1) * LANES] = (n1[:, span] + picked).astype(BF16)
    loads[2].wait()
    total = 0.0
    for lo, size in tiles(edges):
        msg = forward(1, lo, size)
        ue[lo : lo + size, :] = (x1[lo : lo + size, 0:d].astype(F32) + msg).astype(BF16)
        total += mm(recv_t[:, lo : lo + size], msg.astype(BF16))
    x2[:, 2 * d : 3 * d] = total.astype(BF16)

    loads[3].wait()
    for lo, size in tiles(nodes):
        out = forward(2, lo, size)
        um[lo : lo + size, :] = (mn[lo : lo + size, :].astype(F32) + out).astype(BF16)
        backward(2, lo, size, mc[lo : lo + size, :].astype(F32))

    blocks = nlat * nlon
    steps = bits_of(nlat) + bits_of(nlon)
    first_rows = x0.shape[1] // nlat
    second_rows = d // nlat
    block_cols = d // nlon

    def place_of(order, l, c):
        at = 0
        for axis, bit in order:
            at = at * 2 + (((l if axis == "lat" else c) >> bit) & 1)
        return at

    def make_grads(k):
        width = 256
        for top in range(0, d, width):
            left = mm(pgs[k][:, top : top + width], xs[k][...], 0, 0).astype(BF16)
            right = mm(ogs[k][:, top : top + width], hs[k][...], 0, 0).astype(BF16)
            for g, (lo, hi, order) in enumerate(groups):
                for l in range(nlat):
                    for i in range(width // block_cols):
                        at = place_of(order, l, top // block_cols + i)
                        cols = slice(i * block_cols, (i + 1) * block_cols)
                        end = min(hi, first_rows)
                        if lo < end:
                            g_refs[g][k, at, :, 0 : end - lo] = left[
                                cols, l * first_rows + lo : l * first_rows + end
                            ]
                        start = max(lo, first_rows)
                        if start < hi:
                            g_refs[g][k, at, :, start - lo : hi - lo] = right[
                                cols,
                                l * second_rows + start - first_rows : l * second_rows + hi - first_rows,
                            ]

    def bit_at(order, i):
        axis, bit = order[i]
        return lax.rem((lat if axis == "lat" else lon) // (1 << bit), 2)

    bases = []
    for lo, hi, order in groups:
        base = [0]
        for i in range(steps):
            base.append(base[i] + bit_at(order, i) * (blocks >> (i + 1)))
        bases.append(base)

    def red_copy(k, g, i):
        order = groups[g][2]
        half = blocks >> (i + 1)
        axis, bit = order[i]
        mine = bit_at(order, i)
        shift = (1 - 2 * mine) * (1 << bit)
        peer = (lat + shift, lon) if axis == "lat" else (lat, lon + shift)
        return pltpu.make_async_remote_copy(
            src_ref=g_refs[g].at[k, pl.ds(bases[g][i] + (1 - mine) * half, half)],
            dst_ref=r_refs[g].at[k, pl.ds(blocks - 2 * half, half)],
            send_sem=red_send.at[k, g, i],
            recv_sem=red_recv.at[k, g, i],
            device_id=peer,
            device_id_type=MESH,
        )

    def add(k, g, i, start, count):
        half = blocks >> (i + 1)
        base, landed = bases[g][i + 1], blocks - 2 * half

        def one(j, carry):
            g_refs[g][k, base + start + j] = (
                g_refs[g][k, base + start + j].astype(F32)
                + r_refs[g][k, landed + start + j].astype(F32)
            ).astype(BF16)
            return carry

        lax.fori_loop(0, count, one, 0)

    def progress(k, g, i):
        red_copy(k, g, i).wait_recv()
        if i + 1 < steps:
            quarter = blocks >> (i + 2)
            mine = bit_at(groups[g][2], i + 1)
            add(k, g, i, (1 - mine) * quarter, quarter)
            red_copy(k, g, i + 1).start()
            add(k, g, i, mine * quarter, quarter)
        else:
            lo, hi, _ = groups[g]
            gout[k, :, lo:hi] = (
                g_refs[g][k, bases[g][steps]].astype(F32) + r_refs[g][k, blocks - 2].astype(F32)
            )

    make_grads(2)
    for g in range(ngroups):
        red_copy(2, g, 0).start()

    loads[4].wait()
    sums_cot = mm(pg2[...], wf[2, d : 3 * d, :], 1, 1).astype(BF16)
    for lo, size in tiles(edges):
        back = mm(recv_t[:, lo : lo + size], sums_cot[:, d : 2 * d], 0, 0)
        backward(1, lo, size, ec[lo : lo + size, :].astype(F32) + back)
    make_grads(1)
    for g in range(ngroups):
        red_copy(1, g, 0).start()
    for g in range(ngroups):
        progress(2, g, 0)
    for lo, size in tiles(slots):
        backward(0, lo, size, mm(grid_t[:, lo : lo + size], sums_cot[:, 0:d], 0, 0))
    make_grads(0)
    for g in range(ngroups):
        red_copy(0, g, 0).start()
    at = {2: 1, 1: 0, 0: 0}
    while min(at.values()) < steps:
        for k in (2, 1, 0):
            if at[k] < steps:
                for g in range(ngroups):
                    progress(k, g, at[k])
                at[k] += 1

    for o in remote_slots:
        def gone(o=o):
            slot_copy(o, 0).wait_send()
            slot_copy(o, 1).wait_send()
        when(o // 3 - 1, gone)
    for side in range(4):
        when(side_a[side], lambda side=side: side_copy(side).wait_send())
    for s in range(1, nlon):
        row_copy(s).wait_send()
    for s in range(1, nlat):
        col_copy(s, False).wait_send()
    for k in range(3):
        for g in range(ngroups):
            for i in range(steps):
                red_copy(k, g, i).wait_send()


def shards(
    nlat, nlon,
    grid_nodes, grid_edges, grid_sender, owner_index, mesh_nodes, mesh_edges, mesh_sender,
    mesh_receiver, w_first, first_bias, w_second, norm_gain, mesh_cotangent, edge_cotangent,
):
    d = grid_nodes.shape[1]
    slots, nodes, edges = grid_edges.shape[0], mesh_nodes.shape[0], mesh_edges.shape[0]
    fin = w_first.shape[1]
    blocks = nlat * nlon
    steps = bits_of(nlat) + bits_of(nlon)
    lanes = (fin + d) // nlat
    groups = plan(nlat, nlon, lanes)
    ngroups = len(groups)
    cols = d // nlon
    rows = (slots, edges, nodes)
    vmem = pl.BlockSpec(memory_space=pltpu.VMEM)
    hbm = pl.BlockSpec(memory_space=pl.ANY)
    per_dev = K_COARSE * d // LANES
    dma = pltpu.SemaphoreType.DMA
    scratch = [pltpu.VMEM((3, blocks, cols, hi - lo), BF16) for lo, hi, _ in groups]
    scratch += [pltpu.VMEM((3, blocks - 1, cols, hi - lo), BF16) for lo, hi, _ in groups]
    scratch += [pltpu.VMEM((slots, d), BF16)]
    scratch += [pltpu.VMEM((r, fin), BF16) for r in rows]
    scratch += [pltpu.VMEM((4 * BORDER, d), BF16), pltpu.VMEM((blocks * per_dev, LANES), BF16)]
    scratch += [pltpu.VMEM((r, d), BF16) for r in rows]
    scratch += [pltpu.VMEM((r, d), F32) for r in rows]
    scratch += [pltpu.VMEM((r, d), F32) for r in rows]
    scratch += [pltpu.VMEM((r, 1), F32) for r in rows]
    scratch += [pltpu.VMEM((r, d), BF16) for r in rows]
    scratch += [pltpu.VMEM((r, d), BF16) for r in rows]
    scratch += [
        pltpu.VMEM(w_first.shape, BF16), pltpu.VMEM(w_second.shape, BF16),
        pltpu.VMEM((nodes, d), BF16), pltpu.VMEM((edges, d), BF16),
    ]
    scratch += [
        dma((5,)), dma((2, 9)), dma((2, 9)), dma((4,)), dma((4,)), dma((nlon,)), dma((nlon,)),
        dma((nlat,)), dma((nlat,)), dma((3, ngroups, steps)), dma((3, ngroups, steps)),
    ]
    updated_mesh, updated_edges, grads = pl.pallas_call(
        functools.partial(kernel, nlat, nlon, groups),
        out_shape=(
            jax.ShapeDtypeStruct((nodes, d), BF16),
            jax.ShapeDtypeStruct((edges, d), BF16),
            jax.ShapeDtypeStruct((3, cols, lanes), F32),
        ),
        in_specs=[
            vmem, vmem, vmem, vmem, vmem, hbm, vmem, vmem, hbm, vmem, hbm, vmem, hbm, hbm,
        ],
        out_specs=(vmem, vmem, vmem),
        scratch_shapes=scratch,
        compiler_params=pltpu.CompilerParams(
            collective_id=0, has_side_effects=True, vmem_limit_bytes=56 * 1024 * 1024
        ),
    )(
        grid_nodes, grid_edges, grid_sender.reshape(1, slots), owner_index.reshape(1, slots),
        mesh_nodes, mesh_edges, mesh_sender.reshape(1, edges), mesh_receiver.reshape(1, edges),
        w_first, first_bias, w_second, norm_gain, mesh_cotangent, edge_cotangent,
    )
    cut = fin // nlat
    grads = jnp.swapaxes(grads, 1, 2)
    return updated_mesh, updated_edges, grads[:, :cut], grads[:, cut:]


def solution(mesh):
    nlat, nlon = mesh.shape["lat"], mesh.shape["lon"]
    rows, flat = P(("lat", "lon"), None), P(("lat", "lon"))
    return jax.shard_map(
        functools.partial(shards, nlat, nlon),
        mesh=mesh,
        in_specs=(
            rows, rows, flat, flat, rows, rows, flat, flat, P(), P(), P(), P(), rows, rows,
        ),
        out_specs=(rows, rows, P(None, "lat", "lon"), P(None, "lat", "lon")),
        check_vma=False,
    )
```

time: 309 us -> 72.4 us (0.23)
  waiting for transfers between devices: 167 us -> 0 us
  Pallas kernels: 0 us -> 62.1 us
  blocking collectives: 39.8 us -> 0 us
  matrix products: 23.5 us -> 0 us
  local copies, waits for them, and re-layouts: 29.3 us -> 9.26 us
  other arithmetic: 19 us -> 0 us
  between operations: 15 us -> 0.64 us
  starting transfers between devices: 14.1 us -> 0 us
    reduce_scatter x2 -> x0, waiting for transfers between devices: 103 us -> none  [the longest x1 84.5 us: shards(): lax.psum_scatter(first_term.astype(jnp.bfloat16), 'lat', scatter_dimensio...]
    pallas_call x0 -> x1, Pallas kernels: none -> 62.1 us  [shards(): pl.pallas_call(functools.partial(kernel, nlat, nlon, groups), out_shape=(...]
    unnamed x4 -> x0, waiting for transfers between devices: 59.4 us -> none
    all_gather x1 -> x0, blocking collectives: 39.8 us -> none  [shards(): lax.all_gather(mesh_nodes[mesh_nodes.shape[0] - K_COARSE:], ('lat', 'lon'...]
    dot_general x18 -> x0, matrix products: 23.5 us -> none  [the longest x3 11.8 us: forward_backward(): lax.dot_general(inputs, pre_grad, (((0,), (0,)), ((), ())), preferred_ele...]
    ppermute x8 -> x0, starting transfers between devices: 13.9 us -> none  [the longest x4 8.31 us: with_halo(): lax.ppermute(head, axis, [((i + 1) % count, i) for i in range(ends)])]
    gather x4 -> x0, local copies, waits for them, and re-layouts: 9.26 us -> none  [the longest x1 2.64 us: layer_pass(): jnp.take(sender_table, edge_senders, axis=0)]
    unnamed x77 -> x2, local copies, waits for them, and re-layouts: 12.2 us -> 3.54 us
  transfers between devices with their start and end apart: 11 -> 0, of which waited for: 4 -> 0; matrix products, arithmetic and copies ran while one was open for 16% -> 0% of each run, Pallas kernels for 0% -> 0%
where the time goes in v1:
time: 72.4 us; the launch traced here: 72 us
  Pallas kernels  62.1 us (86%)
  local copies, waits for them, and re-layouts  9.26 us (13%)
    pallas_call x1, Pallas kernels, shards(): pl.pallas_call(functools.partial(kernel, nlat, nlon, groups), out_shape=(...  62.1 us
    unnamed x2, local copies, waits for them, and re-layouts  3.54 us
    slice x2, local copies, waits for them, and re-layouts, shards(): return (updated_mesh, updated_edges, grads[:, :cut], grads[:, cut:])  3.23 us

profile of v1, /device:TPU:0, one launch (start us, length us, event | category | flops | bytes accessed | tf_op | source)
XLA Modules:
  0.0 72.0 jit_solution(15287058952904953942)
XLA Ops:
  0.6 1.2 %reshape.20.refs_2_ = s32[1,288]{1,0:T(1,128)} reshape(s32[288]{0:T(512)} %param.16) | data formatting | bytes 2304 | tf_op jit(solution)/shard_map/reshape | solution.py:467
  1.9 1.2 %reshape.21.refs_3_ = s32[1,288]{1,0:T(1,128)} reshape(s32[288]{0:T(512)} %param.17) | data formatting | bytes 2304 | tf_op jit(solution)/shard_map/reshape | solution.py:467
  3.1 62.1 %shard_map.165 = (bf16[256,512]{1,0:T(8,128)(2,1)}, bf16[512,512]{1,0:T(8,128)(2,1)}, f32[3,64,512]{2,1,0:T(8,128)}) custom-call(bf16[1024,512]{1,0:T(8,128)(2,1)} %refs_0_.1, bf16[288,512]{1,0:T(8,128)(2,1)} %refs_1_.1, s32[1,288]{1,0:T(1,128)} %reshape.20.refs_2_, s32[1,288]{1,0:T(1,128)} %reshape.21.refs_3_, bf16[256,512]{1,0:T(8,128)(2,1)} %refs_4_.1, ...), custom_call_target="tpu_custom_call" | custom-call | tf_op jit(solution)/shard_map/pallas_call | solution.py:451
  65.3 1.5 %slice.9 = f32[3,128,64]{1,2,0:T(8,128)} slice(f32[3,512,64]{1,2,0:T(8,128)} %bitcast.3), slice={[0:3], [384:512], [0:64]} | slice | bytes 196608 | tf_op jit(solution)/shard_map/slice | solution.py:473
  66.8 1.7 %slice.8 = f32[3,384,64]{1,2,0:T(8,128)} slice(f32[3,512,64]{1,2,0:T(8,128)} %bitcast.4), slice={[0:3], [0:384], [0:64]} | slice | bytes 589824 | tf_op jit(solution)/shard_map/slice | solution.py:473
  68.5 1.7 %copy.20 = bf16[256,512]{1,0:T(8,128)(2,1)} copy(bf16[256,512]{1,0:T(8,128)(2,1)} %get-tuple-element.14) | data formatting | bytes 524288
  70.2 1.9 %copy.21 = bf16[512,512]{1,0:T(8,128)(2,1)} copy(bf16[512,512]{1,0:T(8,128)(2,1)} %get-tuple-element.15) | data formatting | bytes 1048576

commit v2 on v1

v2 whole, which is shorter than its diff:
```python
import functools

import jax
import jax.numpy as jnp
from jax import lax
from jax.experimental import pallas as pl
from jax.experimental.pallas import tpu as pltpu
from jax.sharding import PartitionSpec as P

BORDER = 64
K_COARSE = 4
EPSILON = 1e-05
LANES = 128
MESH = pl.DeviceIdType.MESH
F32 = jnp.float32
BF16 = jnp.bfloat16


def mm(a, b, ca=1, cb=0):
    return lax.dot_general(a, b, (((ca,), (cb,)), ((), ())), preferred_element_type=F32)


def onehot_t(index, count):
    rows = lax.broadcasted_iota(jnp.int32, (count, index.shape[1]), 0)
    return jnp.where(rows == index, 1.0, 0.0).astype(BF16)


def bits_of(count):
    return count.bit_length() - 1


def plan(nlat, nlon, lanes):
    lat = [("lat", b) for b in range(bits_of(nlat))]
    lon = [("lon", b) for b in range(bits_of(nlon))]
    core, rest = lon[:1], lon[1:]
    x_first = core + rest + lat
    y_first = core + rest[1:] + lat + rest[:1]
    z_first = core + lat + rest
    spare = (x_first, y_first, x_first)
    units = max(lanes // LANES, 1)
    cycle = (z_first, y_first, x_first)
    return [
        [spare[k] if u % 4 == 3 else cycle[u % 4] for u in range(units)] for k in range(3)
    ]


def kernel(nlat, nlon, orders, *refs):
    (gn_h, ge_h, gs, ow, mn_h, me_h, ms, mr, wf_h, fb, ws_h, ng, mc_h, ec_h) = refs[:14]
    (um_h, ue_h, gout) = refs[14:17]
    (
        grads, landed, um, ue, gn, mn,
        snd, x0, x1, x2, bord, coarse,
        h0, h1, h2, p0, p1, p2, n0, n1, n2, r0, r1, r2,
        pg0, pg1, pg2, og0, og1, og2,
        wf, ws, mc, ec,
        load_sem, slot_send, slot_recv, side_send, side_recv, row_send, row_recv, col_send, col_recv,
        red_send, red_recv,
    ) = refs[17:]
    units = len(orders[0])
    gs_row, ow_row = gs[...].reshape(1, gs.shape[0]), ow[...].reshape(1, ow.shape[0])
    ms_row, mr_row = ms[...].reshape(1, ms.shape[0]), mr[...].reshape(1, mr.shape[0])
    xs, hs, ps, ns, rs = (x0, x1, x2), (h0, h1, h2), (p0, p1, p2), (n0, n1, n2), (r0, r1, r2)
    pgs, ogs = (pg0, pg1, pg2), (og0, og1, og2)
    lat, lon = lax.axis_index("lat"), lax.axis_index("lon")
    nodes, d = mn.shape
    slots = ge_h.shape[0]
    cap = slots // 9
    edges = ue.shape[0]
    has = {-1: lat > 0, 1: lat < nlat - 1}

    def when(a, action):
        if a == 0:
            action()
        else:
            pl.when(has[a])(action)

    barrier = pltpu.get_barrier_semaphore()
    peers = [(lat, lax.rem(lon + s, nlon)) for s in range(1, nlon)]
    peers += [(lax.rem(lat + s, nlat), lon) for s in range(1, nlat)]
    peers += [
        (lax.rem(lat + a, nlat), lax.rem(lon + b, nlon))
        for a in (1, nlat - 1)
        for b in (1, nlon - 1)
    ]
    for peer in peers:
        pl.semaphore_signal(barrier, inc=1, device_id=peer, device_id_type=MESH)

    loads = [
        pltpu.make_async_copy(gn_h, gn, load_sem.at[0]),
        pltpu.make_async_copy(mn_h, mn, load_sem.at[1]),
        pltpu.make_async_copy(me_h, x1.at[:, pl.ds(0, d)], load_sem.at[2]),
        pltpu.make_async_copy(wf_h, wf, load_sem.at[3]),
        pltpu.make_async_copy(ws_h, ws, load_sem.at[4]),
        pltpu.make_async_copy(mc_h, mc, load_sem.at[5]),
        pltpu.make_async_copy(ec_h, ec, load_sem.at[6]),
        pltpu.make_async_copy(
            ge_h.at[pl.ds(4 * cap, cap)], x0.at[pl.ds(4 * cap, cap), pl.ds(0, d)], load_sem.at[7]
        ),
    ]
    for copy in loads:
        copy.start()

    loads[0].wait()
    snd[...] = mm(onehot_t(gs_row, gn.shape[0]), gn[...], 0, 0).astype(BF16)
    loads[1].wait()
    per_dev = K_COARSE * d // LANES
    tail = mn[nodes - 16 : nodes, :]
    out_row = lax.broadcasted_iota(jnp.int32, (per_dev, 16), 0)
    in_row = lax.broadcasted_iota(jnp.int32, (per_dev, 16), 1)
    staged = jnp.zeros((per_dev, LANES), F32)
    for q in range(d // LANES):
        pick = (out_row - q * K_COARSE == in_row - (16 - K_COARSE)) & (in_row >= 16 - K_COARSE)
        staged += mm(jnp.where(pick, 1.0, 0.0).astype(BF16), tail[:, q * LANES : (q + 1) * LANES])
    me_row = (lon * nlat + lat) * per_dev
    coarse[pl.ds(pl.multiple_of(me_row, 16), per_dev), :] = staged.astype(BF16)

    @pl.when(lat == 0)
    def _():
        x0[0 : 3 * cap, 0 : 2 * d] = jnp.zeros((3 * cap, 2 * d), BF16)
        bord[0:BORDER, :] = jnp.zeros((BORDER, d), BF16)

    @pl.when(lat == nlat - 1)
    def _():
        x0[6 * cap : 9 * cap, 0 : 2 * d] = jnp.zeros((3 * cap, 2 * d), BF16)
        bord[BORDER : 2 * BORDER, :] = jnp.zeros((BORDER, d), BF16)

    pl.semaphore_wait(barrier, len(peers))

    def slot_copy(o, part):
        a, b = o // 3 - 1, o % 3 - 1
        src = (ge_h, snd)[part]
        return pltpu.make_async_remote_copy(
            src_ref=src.at[pl.ds(o * cap, cap)],
            dst_ref=x0.at[pl.ds((8 - o) * cap, cap), pl.ds(part * d, d)],
            send_sem=slot_send.at[part, o],
            recv_sem=slot_recv.at[part, 8 - o],
            device_id=(lat + a, lax.rem(lon + b + nlon, nlon)),
            device_id_type=MESH,
        )

    def side_copy(side):
        a, b = ((1, 0), (-1, 0), (0, 1), (0, -1))[side]
        return pltpu.make_async_remote_copy(
            src_ref=mn.at[pl.ds(0, BORDER)],
            dst_ref=bord.at[pl.ds(side * BORDER, BORDER)],
            send_sem=side_send.at[side],
            recv_sem=side_recv.at[side],
            device_id=(lat + a, lax.rem(lon + b + nlon, nlon)),
            device_id_type=MESH,
        )

    side_a = (1, -1, 0, 0)
    def col_copy(s, incoming):
        other = lax.rem(lat - s + nlat, nlat) if incoming else lax.rem(lat + s, nlat)
        owner = other if incoming else lat
        span = pl.ds(pl.multiple_of((lon * nlat + owner) * per_dev, 16), per_dev)
        return pltpu.make_async_remote_copy(
            src_ref=coarse.at[span], dst_ref=coarse.at[span],
            send_sem=col_send.at[s], recv_sem=col_recv.at[s],
            device_id=(other, lon), device_id_type=MESH,
        )

    def row_copy(s, incoming):
        other = lax.rem(lon - s + nlon, nlon) if incoming else lax.rem(lon + s, nlon)
        owner = other if incoming else lon
        span = pl.ds(pl.multiple_of(owner * nlat * per_dev, 16), nlat * per_dev)
        return pltpu.make_async_remote_copy(
            src_ref=coarse.at[span], dst_ref=coarse.at[span],
            send_sem=row_send.at[s], recv_sem=row_recv.at[s],
            device_id=(lat, other), device_id_type=MESH,
        )

    remote_slots = [0, 2, 6, 8, 1, 7, 3, 5]
    for s in range(1, nlat):
        col_copy(s, False).start()
    for side in range(4):
        when(side_a[side], lambda side=side: side_copy(side).start())
    for part in (1, 0):
        for o in remote_slots:
            when(o // 3 - 1, lambda o=o, part=part: slot_copy(o, part).start())

    recv_t = onehot_t(mr_row, nodes)
    x1[:, 2 * d : 3 * d] = mm(recv_t, mn[...], 0, 0).astype(BF16)
    for s in range(1, nlat):
        col_copy(s, True).wait_recv()
    for s in range(1, nlon):
        row_copy(s, False).start()
    n1[...] = mm(onehot_t(ms_row, nodes), mn[...], 0, 0)
    x0[4 * cap : 5 * cap, d : 2 * d] = snd[4 * cap : 5 * cap, :]
    own_t = onehot_t(jnp.maximum(ow_row, 0), nodes)
    x0[:, 2 * d : 3 * d] = mm(own_t, mn[...], 0, 0).astype(BF16)
    x2[:, 0:d] = mn[...]
    loads[2].wait()
    loads[3].wait()
    p1[...] = (
        mm(x1[:, 0:d], wf[1, 0:d, :])
        + mm(x1[:, 2 * d : 3 * d], wf[1, 2 * d : 3 * d, :])
        + fb[1:2, :]
    )
    p0[...] = mm(x0[:, 2 * d : 3 * d], wf[0, 2 * d : 3 * d, :]) + fb[0:1, :]
    p2[...] = mm(mn[...], wf[2, 0:d, :]) + fb[2:3, :]
    loads[4].wait()
    late = ((0, 2 * d), (d, 2 * d), (d, 3 * d))

    def forward(k, lo, size):
        rows = pl.ds(lo, size)
        lo_in, hi_in = late[k]
        pre = ps[k][rows, :] + mm(xs[k][rows, lo_in:hi_in], wf[k, lo_in:hi_in, :])
        ps[k][rows, :] = pre
        hidden = (pre * jax.nn.sigmoid(pre)).astype(BF16)
        hs[k][rows, :] = hidden
        out = mm(hidden, ws[k])
        centred = out - jnp.mean(out, axis=-1, keepdims=True)
        scale = lax.rsqrt(jnp.mean(centred * centred, axis=-1, keepdims=True) + EPSILON)
        normed = centred * scale
        ns[k][rows, :] = normed
        rs[k][rows, :] = scale
        return normed * ng[k : k + 1, :]

    def backward(k, lo, size, dmsg):
        rows = pl.ds(lo, size)
        dn = dmsg * ng[k : k + 1, :]
        normed = ns[k][rows, :]
        dout = rs[k][rows, :] * (
            dn
            - jnp.mean(dn, axis=-1, keepdims=True)
            - normed * jnp.mean(dn * normed, axis=-1, keepdims=True)
        )
        og = dout.astype(BF16)
        ogs[k][rows, :] = og
        dh = mm(og, ws[k], 1, 1).astype(BF16).astype(F32)
        pre = ps[k][rows, :]
        gate = jax.nn.sigmoid(pre)
        pg = (dh * (gate * (1.0 + pre * (1.0 - gate)))).astype(BF16)
        pgs[k][rows, :] = pg
        return pg

    def tiles(count):
        size = 256 if count % 256 == 0 else count
        return [(i * size, size) for i in range(count // size)]

    for side in range(4):
        when(-side_a[side], lambda side=side: side_copy(side).wait_recv())
    n1[...] += mm(onehot_t(ms_row - nodes, 4 * BORDER), bord[...], 0, 0)
    for s in range(1, nlon):
        row_copy(s, True).wait_recv()
    rank = ms_row - (nodes + 4 * BORDER)
    owner = lax.shift_right_logical(rank, bits_of(K_COARSE))
    owner = (owner & (nlon - 1)) * nlat + lax.shift_right_logical(owner, bits_of(nlon))
    place = owner * per_dev + (rank & (K_COARSE - 1))
    for q in range(d // LANES):
        target = jnp.where(rank >= 0, place + q * K_COARSE, -1)
        picked = mm(onehot_t(target, coarse.shape[0]), coarse[...], 0, 0)
        span = slice(q * LANES, (q + 1) * LANES)
        x1[:, d + q * LANES : d + (q + 1) * LANES] = (n1[:, span] + picked).astype(BF16)
    total = 0.0
    for lo, size in tiles(edges):
        msg = forward(1, lo, size)
        ue[lo : lo + size, :] = (x1[lo : lo + size, 0:d].astype(F32) + msg).astype(BF16)
        total += mm(recv_t[:, lo : lo + size], msg.astype(BF16))
    x2[:, 2 * d : 3 * d] = total.astype(BF16)

    ue_out = pltpu.make_async_copy(ue, ue_h, load_sem.at[8])
    ue_out.start()

    loads[7].wait()
    for j in remote_slots:
        def arrive(j=j):
            slot_copy(8 - j, 0).wait_recv()
            slot_copy(8 - j, 1).wait_recv()
        when(j // 3 - 1, arrive)
    grid_msgs = [forward(0, lo, size).astype(BF16) for lo, size in tiles(slots)]
    grid_t = onehot_t(ow_row, nodes)
    total = 0.0
    for (lo, size), msg in zip(tiles(slots), grid_msgs):
        total += mm(grid_t[:, lo : lo + size], msg)
    x2[:, d : 2 * d] = total.astype(BF16)

    loads[5].wait()
    for lo, size in tiles(nodes):
        out = forward(2, lo, size)
        um[lo : lo + size, :] = (mn[lo : lo + size, :].astype(F32) + out).astype(BF16)
        backward(2, lo, size, mc[lo : lo + size, :].astype(F32))

    um_out = pltpu.make_async_copy(um, um_h, load_sem.at[9])
    um_out.start()

    blocks = nlat * nlon
    steps = bits_of(nlat) + bits_of(nlon)
    first_rows = x0.shape[1] // nlat
    second_rows = d // nlat
    block_cols = d // nlon
    unit = gout.shape[2] // units

    def place_of(order, l, c):
        at = 0
        for axis, bit in order:
            at = at * 2 + (((l if axis == "lat" else c) >> bit) & 1)
        return at

    def make_grads(k):
        width = 256
        for top in range(0, d, width):
            left = mm(pgs[k][:, top : top + width], xs[k][...], 0, 0).astype(BF16)
            right = mm(ogs[k][:, top : top + width], hs[k][...], 0, 0).astype(BF16)
            for u, order in enumerate(orders[k]):
                lo, hi = u * unit, (u + 1) * unit
                end, start = min(hi, first_rows), max(lo, first_rows)
                for l in range(nlat):
                    for i in range(width // block_cols):
                        at = place_of(order, l, top // block_cols + i)
                        cols = slice(i * block_cols, (i + 1) * block_cols)
                        if lo < end:
                            span = slice(l * first_rows + lo, l * first_rows + end)
                            grads[k, u, at, :, 0 : end - lo] = left[cols, span]
                        if start < hi:
                            from_row = l * second_rows - first_rows
                            span = slice(from_row + start, from_row + hi)
                            grads[k, u, at, :, start - lo : unit] = right[cols, span]

    def bit_at(order, i):
        axis, bit = order[i]
        return lax.rem((lat if axis == "lat" else lon) // (1 << bit), 2)

    def base_of(order, i):
        base = 0
        for step in range(i):
            base = base + bit_at(order, step) * (blocks >> (step + 1))
        return base

    def red_copy(k, u, i):
        order = orders[k][u]
        half = blocks >> (i + 1)
        axis, bit = order[i]
        mine = bit_at(order, i)
        shift = (1 - 2 * mine) * (1 << bit)
        peer = (lat + shift, lon) if axis == "lat" else (lat, lon + shift)
        return pltpu.make_async_remote_copy(
            src_ref=grads.at[k, u, pl.ds(base_of(order, i) + (1 - mine) * half, half)],
            dst_ref=landed.at[k, u, pl.ds(blocks - 2 * half, half)],
            send_sem=red_send.at[k, u, i],
            recv_sem=red_recv.at[k, u, i],
            device_id=peer,
            device_id_type=MESH,
        )

    def add(k, u, i, start, count):
        half = blocks >> (i + 1)
        base, from_block = base_of(orders[k][u], i + 1) + start, blocks - 2 * half + start

        def one(j, carry):
            grads[k, u, base + j] = grads[k, u, base + j] + landed[k, u, from_block + j]
            return carry

        lax.fori_loop(0, count, one, 0)

    def progress(k, i):
        for u in range(units):
            red_copy(k, u, i).wait_recv()
            if i + 1 < steps:
                quarter = blocks >> (i + 2)
                mine = bit_at(orders[k][u], i + 1)
                add(k, u, i, (1 - mine) * quarter, quarter)
                red_copy(k, u, i + 1).start()
                add(k, u, i, mine * quarter, quarter)
            else:
                gout[k, :, u * unit : (u + 1) * unit] = (
                    grads[k, u, base_of(orders[k][u], steps)].astype(F32)
                    + landed[k, u, blocks - 2].astype(F32)
                )

    def begin(k):
        make_grads(k)
        for u in range(units):
            red_copy(k, u, 0).start()

    begin(2)
    loads[6].wait()
    sums_cot = mm(pg2[...], wf[2, d : 3 * d, :], 1, 1).astype(BF16)
    for n, (lo, size) in enumerate(tiles(edges)):
        back = mm(recv_t[:, lo : lo + size], sums_cot[:, d : 2 * d], 0, 0)
        backward(1, lo, size, ec[lo : lo + size, :].astype(F32) + back)
        if n == 0:
            progress(2, 0)
    begin(1)
    for lo, size in tiles(slots):
        backward(0, lo, size, mm(grid_t[:, lo : lo + size], sums_cot[:, 0:d], 0, 0))
    progress(1, 0)
    begin(0)
    progress(2, 1)
    progress(0, 0)
    rest = [(i - k, -k, k, i) for k in range(3) for i in range(2 if k == 2 else 1, steps)]
    for _, _, k, i in sorted(rest):
        progress(k, i)

    ue_out.wait()
    um_out.wait()
    for o in remote_slots:
        def gone(o=o):
            slot_copy(o, 0).wait_send()
            slot_copy(o, 1).wait_send()
        when(o // 3 - 1, gone)
    for side in range(4):
        when(side_a[side], lambda side=side: side_copy(side).wait_send())
    for s in range(1, nlon):
        row_copy(s, False).wait_send()
    for s in range(1, nlat):
        col_copy(s, False).wait_send()
    for k in range(3):
        for u in range(units):
            for i in range(steps):
                red_copy(k, u, i).wait_send()


def hand_over(cut, um_in, ue_in, grads_in, um, ue, first, second, sems):
    copies = [
        pltpu.make_async_copy(um_in, um, sems.at[0]),
        pltpu.make_async_copy(ue_in, ue, sems.at[1]),
        pltpu.make_async_copy(grads_in.at[:, :, pl.ds(0, cut)], first, sems.at[2]),
        pltpu.make_async_copy(
            grads_in.at[:, :, pl.ds(cut, second.shape[2])], second, sems.at[3]
        ),
    ]
    for copy in copies:
        copy.start()
    for copy in copies:
        copy.wait()


def shards(
    nlat, nlon,
    grid_nodes, grid_edges, grid_sender, owner_index, mesh_nodes, mesh_edges, mesh_sender,
    mesh_receiver, w_first, first_bias, w_second, norm_gain, mesh_cotangent, edge_cotangent,
):
    d = grid_nodes.shape[1]
    slots, nodes, edges = grid_edges.shape[0], mesh_nodes.shape[0], mesh_edges.shape[0]
    fin = w_first.shape[1]
    blocks = nlat * nlon
    steps = bits_of(nlat) + bits_of(nlon)
    lanes = (fin + d) // nlat
    orders = plan(nlat, nlon, lanes)
    units = len(orders[0])
    cols = d // nlon
    rows = (slots, edges, nodes)
    vmem = pl.BlockSpec(memory_space=pltpu.VMEM)
    hbm = pl.BlockSpec(memory_space=pl.ANY)
    per_dev = K_COARSE * d // LANES
    dma = pltpu.SemaphoreType.DMA
    scratch = [
        pltpu.VMEM((3, units, blocks, cols, lanes // units), BF16),
        pltpu.VMEM((3, units, blocks - 1, cols, lanes // units), BF16),
        pltpu.VMEM((nodes, d), BF16), pltpu.VMEM((edges, d), BF16),
        pltpu.VMEM(grid_nodes.shape, BF16), pltpu.VMEM((nodes, d), BF16),
    ]
    scratch += [pltpu.VMEM((slots, d), BF16)]
    scratch += [pltpu.VMEM((r, fin), BF16) for r in rows]
    scratch += [pltpu.VMEM((4 * BORDER, d), BF16), pltpu.VMEM((blocks * per_dev, LANES), BF16)]
    scratch += [pltpu.VMEM((r, d), BF16) for r in rows]
    scratch += [pltpu.VMEM((r, d), F32) for r in rows]
    scratch += [pltpu.VMEM((r, d), F32) for r in rows]
    scratch += [pltpu.VMEM((r, 1), F32) for r in rows]
    scratch += [pltpu.VMEM((r, d), BF16) for r in rows]
    scratch += [pltpu.VMEM((r, d), BF16) for r in rows]
    scratch += [
        pltpu.VMEM(w_first.shape, BF16), pltpu.VMEM(w_second.shape, BF16),
        pltpu.VMEM((nodes, d), BF16), pltpu.VMEM((edges, d), BF16),
    ]
    scratch += [
        dma((10,)), dma((2, 9)), dma((2, 9)), dma((4,)), dma((4,)), dma((nlon,)), dma((nlon,)),
        dma((nlat,)), dma((nlat,)), dma((3, units, steps)), dma((3, units, steps)),
    ]
    updated_mesh, updated_edges, grads = pl.pallas_call(
        functools.partial(kernel, nlat, nlon, orders),
        out_shape=(
            jax.ShapeDtypeStruct((nodes, d), BF16),
            jax.ShapeDtypeStruct((edges, d), BF16),
            jax.ShapeDtypeStruct((3, cols, lanes), F32),
        ),
        in_specs=[
            hbm, hbm, vmem, vmem, hbm, hbm, vmem, vmem, hbm, vmem, hbm, vmem, hbm, hbm,
        ],
        out_specs=(hbm, hbm, vmem),
        scratch_shapes=scratch,
        compiler_params=pltpu.CompilerParams(
            collective_id=0, has_side_effects=True, vmem_limit_bytes=56 * 1024 * 1024
        ),
    )(
        grid_nodes, grid_edges, grid_sender, owner_index, mesh_nodes, mesh_edges,
        mesh_sender, mesh_receiver,
        w_first, first_bias, w_second, norm_gain, mesh_cotangent, edge_cotangent,
    )
    cut = fin // nlat
    if cut % LANES:
        grads = jnp.swapaxes(grads, 1, 2)
        return updated_mesh, updated_edges, grads[:, :cut], grads[:, cut:]
    updated_mesh, updated_edges, first, second = pl.pallas_call(
        functools.partial(hand_over, cut),
        out_shape=(
            jax.ShapeDtypeStruct((nodes, d), BF16),
            jax.ShapeDtypeStruct((edges, d), BF16),
            jax.ShapeDtypeStruct((3, cols, cut), F32),
            jax.ShapeDtypeStruct((3, cols, lanes - cut), F32),
        ),
        in_specs=[hbm, hbm, hbm],
        out_specs=(hbm, hbm, hbm, hbm),
        scratch_shapes=[dma((4,))],
    )(updated_mesh, updated_edges, grads)
    return updated_mesh, updated_edges, jnp.swapaxes(first, 1, 2), jnp.swapaxes(second, 1, 2)


def solution(mesh):
    nlat, nlon = mesh.shape["lat"], mesh.shape["lon"]
    rows, flat = P(("lat", "lon"), None), P(("lat", "lon"))
    return jax.shard_map(
        functools.partial(shards, nlat, nlon),
        mesh=mesh,
        in_specs=(
            rows, rows, flat, flat, rows, rows, flat, flat, P(), P(), P(), P(), rows, rows,
        ),
        out_specs=(rows, rows, P(None, "lat", "lon"), P(None, "lat", "lon")),
        check_vma=False,
    )
```

time: 72.4 us -> 99.3 us (1.37)
  Pallas kernels: 62.1 us -> 98.4 us
  local copies, waits for them, and re-layouts: 9.26 us -> 0 us
    pallas_call x1 -> x2, Pallas kernels: 62.1 us -> 98.4 us  [the longest x1 61.6 us: shards(): pl.pallas_call(functools.partial(kernel, nlat, nlon, orders), out_shape=(...]
    unnamed x2 -> x0, local copies, waits for them, and re-layouts: 3.54 us -> none
    slice x2 -> x0, local copies, waits for them, and re-layouts: 3.23 us -> none  [shards(): return (updated_mesh, updated_edges, grads[:, :cut], grads[:, cut:])]
    reshape x2 -> x0, local copies, waits for them, and re-layouts: 2.49 us -> none  [the longest x1 1.25 us: shards(): grid_sender.reshape(1, slots)]
where the time goes in v2:
time: 99.3 us; the launch traced here: 99.1 us
  Pallas kernels  98.4 us (99%)
    pallas_call x1, Pallas kernels, shards(): pl.pallas_call(functools.partial(kernel, nlat, nlon, orders), out_shape=(...  61.6 us
    pallas_call x1, Pallas kernels, shards(): pl.pallas_call(functools.partial(hand_over, cut), out_shape=(jax.ShapeDty...  36.9 us

profile of v2, /device:TPU:0, one launch (start us, length us, event | category | flops | bytes accessed | tf_op | source)
XLA Modules:
  0.0 99.1 jit_solution(3588583168911690956)
XLA Ops:
  0.6 61.6 %shard_map.165 = (bf16[256,512]{1,0:T(8,128)(2,1)}, bf16[512,512]{1,0:T(8,128)(2,1)}, f32[3,64,512]{2,1,0:T(8,128)}) custom-call(bf16[1024,512]{1,0:T(8,128)(2,1)} %refs_0_.1, bf16[288,512]{1,0:T(8,128)(2,1)} %refs_1_.1, s32[288]{0:T(512)} %refs_2_.1, s32[288]{0:T(512)} %refs_3_.1, bf16[256,512]{1,0:T(8,128)(2,1)} %refs_4_.1, bf16[512,512]{1,0:T(8,128)(2,1)} %refs_5_.1, ...), custom_call_target="tpu_custom_call" | custom-call | tf_op jit(solution)/shard_map/pallas_call | solution.py:472
  62.2 36.9 %shard_map.166 = (bf16[256,512]{1,0:T(8,128)(2,1)}, bf16[512,512]{1,0:T(8,128)(2,1)}, f32[3,64,384]{2,1,0:T(8,128)}, f32[3,64,128]{2,1,0:T(8,128)}) custom-call(bf16[256,512]{1,0:T(8,128)(2,1)} %get-tuple-element.11.um_in, bf16[512,512]{1,0:T(8,128)(2,1)} %get-tuple-element.12.ue_in, f32[3,64,512]{2,1,0:T(8,128)} %get-tuple-element.13.grads_in), custom_call_target="tpu_custom_call" | custom-call | tf_op jit(solution)/shard_map/pallas_call | solution.py:496

commit v3 on v2

--- a/solution.py
+++ b/solution.py
@@ -57,6 +57,8 @@
         red_send, red_recv,
     ) = refs[17:]
     units = len(orders[0])
+    blocks = nlat * nlon
+    steps = bits_of(nlat) + bits_of(nlon)
     gs_row, ow_row = gs[...].reshape(1, gs.shape[0]), ow[...].reshape(1, ow.shape[0])
     ms_row, mr_row = ms[...].reshape(1, ms.shape[0]), mr[...].reshape(1, mr.shape[0])
     xs, hs, ps, ns, rs = (x0, x1, x2), (h0, h1, h2), (p0, p1, p2), (n0, n1, n2), (r0, r1, r2)
@@ -100,8 +102,6 @@
     for copy in loads:
         copy.start()
 
-    loads[0].wait()
-    snd[...] = mm(onehot_t(gs_row, gn.shape[0]), gn[...], 0, 0).astype(BF16)
     loads[1].wait()
     per_dev = K_COARSE * d // LANES
     tail = mn[nodes - 16 : nodes, :]
@@ -175,9 +175,12 @@
         col_copy(s, False).start()
     for side in range(4):
         when(side_a[side], lambda side=side: side_copy(side).start())
-    for part in (1, 0):
-        for o in remote_slots:
-            when(o // 3 - 1, lambda o=o, part=part: slot_copy(o, part).start())
+    for o in remote_slots:
+        when(o // 3 - 1, lambda o=o: slot_copy(o, 0).start())
+    loads[0].wait()
+    snd[...] = mm(onehot_t(gs_row, gn.shape[0]), gn[...], 0, 0).astype(BF16)
+    for o in remote_slots:
+        when(o // 3 - 1, lambda o=o: slot_copy(o, 1).start())
 
     recv_t = onehot_t(mr_row, nodes)
     x1[:, 2 * d : 3 * d] = mm(recv_t, mn[...], 0, 0).astype(BF16)
@@ -241,18 +244,19 @@
 
     for side in range(4):
         when(-side_a[side], lambda side=side: side_copy(side).wait_recv())
-    n1[...] += mm(onehot_t(ms_row - nodes, 4 * BORDER), bord[...], 0, 0)
     for s in range(1, nlon):
         row_copy(s, True).wait_recv()
-    rank = ms_row - (nodes + 4 * BORDER)
-    owner = lax.shift_right_logical(rank, bits_of(K_COARSE))
+    shape = (blocks * K_COARSE, blocks * per_dev)
+    entry = lax.broadcasted_iota(jnp.int32, shape, 0)
+    packed = lax.broadcasted_iota(jnp.int32, shape, 1)
+    owner = lax.shift_right_logical(entry, bits_of(K_COARSE))
     owner = (owner & (nlon - 1)) * nlat + lax.shift_right_logical(owner, bits_of(nlon))
-    place = owner * per_dev + (rank & (K_COARSE - 1))
+    offset = packed - owner * per_dev - (entry & (K_COARSE - 1))
     for q in range(d // LANES):
-        target = jnp.where(rank >= 0, place + q * K_COARSE, -1)
-        picked = mm(onehot_t(target, coarse.shape[0]), coarse[...], 0, 0)
-        span = slice(q * LANES, (q + 1) * LANES)
-        x1[:, d + q * LANES : d + (q + 1) * LANES] = (n1[:, span] + picked).astype(BF16)
+        pick = jnp.where(offset == q * K_COARSE, 1.0, 0.0).astype(BF16)
+        bord[4 * BORDER :, q * LANES : (q + 1) * LANES] = mm(pick, coarse[...]).astype(BF16)
+    away = mm(onehot_t(ms_row - nodes, bord.shape[0]), bord[...], 0, 0)
+    x1[:, d : 2 * d] = (n1[...] + away).astype(BF16)
     total = 0.0
     for lo, size in tiles(edges):
         msg = forward(1, lo, size)
@@ -285,8 +289,6 @@
     um_out = pltpu.make_async_copy(um, um_h, load_sem.at[9])
     um_out.start()
 
-    blocks = nlat * nlon
-    steps = bits_of(nlat) + bits_of(nlon)
     first_rows = x0.shape[1] // nlat
     second_rows = d // nlat
     block_cols = d // nlon
@@ -348,11 +350,10 @@
         half = blocks >> (i + 1)
         base, from_block = base_of(orders[k][u], i + 1) + start, blocks - 2 * half + start
 
-        def one(j, carry):
-            grads[k, u, base + j] = grads[k, u, base + j] + landed[k, u, from_block + j]
-            return carry
-
-        lax.fori_loop(0, count, one, 0)
+        step = min(count, 8)
+        for j in range(0, count, step):
+            to, frm = pl.ds(base + j, step), pl.ds(from_block + j, step)
+            grads[k, u, to] = grads[k, u, to] + landed[k, u, frm]
 
     def progress(k, i):
         for u in range(units):
@@ -412,19 +413,11 @@
                 red_copy(k, u, i).wait_send()
 
 
-def hand_over(cut, um_in, ue_in, grads_in, um, ue, first, second, sems):
-    copies = [
-        pltpu.make_async_copy(um_in, um, sems.at[0]),
-        pltpu.make_async_copy(ue_in, ue, sems.at[1]),
-        pltpu.make_async_copy(grads_in.at[:, :, pl.ds(0, cut)], first, sems.at[2]),
-        pltpu.make_async_copy(
-            grads_in.at[:, :, pl.ds(cut, second.shape[2])], second, sems.at[3]
-        ),
-    ]
-    for copy in copies:
-        copy.start()
-    for copy in copies:
-        copy.wait()
+def hand_over(cut, um_in, ue_in, grads_in, um, ue, first, second):
+    um[...] = um_in[...]
+    ue[...] = ue_in[...]
+    first[...] = grads_in[:, :, 0:cut]
+    second[...] = grads_in[:, :, cut:]
 
 
 def shards(
@@ -454,7 +447,7 @@
     ]
     scratch += [pltpu.VMEM((slots, d), BF16)]
     scratch += [pltpu.VMEM((r, fin), BF16) for r in rows]
-    scratch += [pltpu.VMEM((4 * BORDER, d), BF16), pltpu.VMEM((blocks * per_dev, LANES), BF16)]
+    scratch += [pltpu.VMEM((4 * BORDER + blocks * K_COARSE, d), BF16), pltpu.VMEM((blocks * per_dev, LANES), BF16)]
     scratch += [pltpu.VMEM((r, d), BF16) for r in rows]
     scratch += [pltpu.VMEM((r, d), F32) for r in rows]
     scratch += [pltpu.VMEM((r, d), F32) for r in rows]
@@ -501,9 +494,8 @@
             jax.ShapeDtypeStruct((3, cols, cut), F32),
             jax.ShapeDtypeStruct((3, cols, lanes - cut), F32),
         ),
-        in_specs=[hbm, hbm, hbm],
-        out_specs=(hbm, hbm, hbm, hbm),
-        scratch_shapes=[dma((4,))],
+        in_specs=[vmem, vmem, vmem],
+        out_specs=(vmem, vmem, vmem, vmem),
     )(updated_mesh, updated_edges, grads)
     return updated_mesh, updated_edges, jnp.swapaxes(first, 1, 2), jnp.swapaxes(second, 1, 2)
 

time: 99.3 us -> 64.4 us (0.65)
  Pallas kernels: 98.4 us -> 63.5 us
    pallas_call x1, Pallas kernels: 36.9 us -> 2.27 us  [shards(): pl.pallas_call(functools.partial(hand_over, cut), out_shape=(jax.ShapeDty...]
where the time goes in v3:
time: 64.4 us; the launch traced here: 64.2 us
  Pallas kernels  63.5 us (99%)
    pallas_call x1, Pallas kernels, shards(): pl.pallas_call(functools.partial(kernel, nlat, nlon, orders), out_shape=(...  61.2 us
    pallas_call x1, Pallas kernels, shards(): pl.pallas_call(functools.partial(hand_over, cut), out_shape=(jax.ShapeDty...  2.27 us

profile of v3, /device:TPU:0, one launch (start us, length us, event | category | flops | bytes accessed | tf_op | source)
XLA Modules:
  0.0 64.2 jit_solution(7843767516787798349)
XLA Ops:
  0.6 61.2 %shard_map.165 = (bf16[256,512]{1,0:T(8,128)(2,1)}, bf16[512,512]{1,0:T(8,128)(2,1)}, f32[3,64,512]{2,1,0:T(8,128)}) custom-call(bf16[1024,512]{1,0:T(8,128)(2,1)} %refs_0_.1, bf16[288,512]{1,0:T(8,128)(2,1)} %refs_1_.1, s32[288]{0:T(512)} %refs_2_.1, s32[288]{0:T(512)} %refs_3_.1, bf16[256,512]{1,0:T(8,128)(2,1)} %refs_4_.1, bf16[512,512]{1,0:T(8,128)(2,1)} %refs_5_.1, ...), custom_call_target="tpu_custom_call" | custom-call | tf_op jit(solution)/shard_map/pallas_call | solution.py:465
  61.9 2.3 %shard_map.166 = (bf16[256,512]{1,0:T(8,128)(2,1)}, bf16[512,512]{1,0:T(8,128)(2,1)}, f32[3,64,384]{2,1,0:T(8,128)}, f32[3,64,128]{2,1,0:T(8,128)}) custom-call(bf16[256,512]{1,0:T(8,128)(2,1)} %get-tuple-element.11.um_in, bf16[512,512]{1,0:T(8,128)(2,1)} %get-tuple-element.12.ue_in, f32[3,64,512]{2,1,0:T(8,128)} %get-tuple-element.13.grads_in), custom_call_target="tpu_custom_call" | custom-call | tf_op jit(solution)/shard_map/pallas_call | solution.py:489
